TPU v7x, 32 devices: a whole 2x2x4 slice. The times are simulated.
32 devices in a mesh: span: 8 (over z, core), chord: 4 (over y, x).
Axes of the slice: x: 2, y: 2, z: 4, core: 2. Of those that a mesh axis runs over, the one named last changes fastest.
Arguments:
- right_side: float32 [16, 256, 512], P(None, 'span', 'chord'), may hold values from -6 to 6
- stiff_scale: float32 [256, 512], P('span', 'chord'), may hold values from 0.5 to 2
- extra_diag: float32 [256, 512], P('span', 'chord'), may hold values from 0.5 to 4
- iface_line: int32 [32], P('chord'), may hold values from 0 to 127, as said below
- partner: int32 [32], P('chord'), may hold values from 0 to 31, as said below
Outputs:
- solution: float32 [16, 256, 512], P(None, 'span', 'chord')
- residual: float32 [16, 256, 512], P(None, 'span', 'chord')
Inputs may be any that keep to these rules, and one draw needn't show every extreme that they name: `iface_line`: each device's 8 entries are distinct; the first two are 0 and 127, the patch's edge lines. partner pairs the slots: partner[partner[q]] = q and partner[q] != q.
All inputs are finite; a program needn't handle non-finite values.
Results may differ from a plain program's by a relative error of at most 0.00016.
Values sent between devices are 32-bit elements; how exact they have to be, the bound alone decides.
A program may use at most 64 MiB of HBM per device.

v0:
```python
import functools

import jax
import jax.numpy as jnp
from jax import lax
from jax.experimental import pallas as pl
from jax.experimental.pallas import tpu as pltpu
from jax.sharding import PartitionSpec as P

mass_taps = (
    1.0 / 5040.0,
    120.0 / 5040.0,
    1191.0 / 5040.0,
    2416.0 / 5040.0,
    1191.0 / 5040.0,
    120.0 / 5040.0,
    1.0 / 5040.0,
)
bend_taps = (1.0 / 6.0, 0.0, -1.5, 8.0 / 3.0, -1.5, 0.0, 1.0 / 6.0)
penalty_weight = 4.0
REACH = 3
LANES = 128
TILE = 8
F32 = jnp.float32
MESH = pl.DeviceIdType.MESH


def dot(a, b, a_dim, b_dim, precision=lax.Precision.HIGH):
    return lax.dot_general(
        a,
        b,
        (((a_dim,), (b_dim,)), ((), ())),
        precision=precision,
        preferred_element_type=F32,
    )


exact_dot = functools.partial(dot, precision=lax.Precision.HIGHEST)


def iota(shape, dim):
    return lax.broadcasted_iota(jnp.int32, shape, dim)


def taps_at(offset, taps):
    out = jnp.zeros(offset.shape, F32)
    for o in range(-REACH, REACH + 1):
        if taps[o + REACH] != 0.0:
            out = jnp.where(offset == o, F32(taps[o + REACH]), out)
    return out


def span_sum(ext_ref, taps, rows):
    total = F32(taps[REACH]) * ext_ref[REACH : REACH + rows]
    for o in range(1, REACH + 1):
        if taps[REACH + o] != 0.0:
            pair = ext_ref[REACH - o : REACH - o + rows] + ext_ref[REACH + o : REACH + o + rows]
            total = total + F32(taps[REACH + o]) * pair
    return total


def eliminate(table, first, count):
    row_at = iota(table.shape, 0)
    columns = [
        jnp.broadcast_to(table[:, first + k : first + k + 1], table.shape) for k in range(count)
    ]
    for k in range(count):
        factor = columns[k]
        inverse = 1.0 / factor[k : k + 1, :]

        def reduce(x):
            row = x[k : k + 1, :] * inverse
            return jnp.where(row_at == k, row, x - factor * row)

        table = reduce(table)
        for j in range(k + 1, count):
            columns[j] = reduce(columns[j])
    return table


def kernel(
    n,
    N,
    right_hbm,
    scale_hbm,
    extra_hbm,
    line_hbm,
    partner_hbm,
    solution_ref,
    residual_ref,
    right_ref,
    scale_ref,
    extra_ref,
    line_ref,
    partner_ref,
    basis,
    weighted,
    halo_out,
    halo,
    iface,
    rim,
    corner,
    ext_m,
    ext_b,
    early_c,
    early_s,
    late_c,
    late_s,
    rim_sems,
    halo_sems,
    corner_sems,
    iface_sems,
    chord_sems,
    span_sems,
    load_sems,
):
    C, R, L = right_ref.shape
    RC = R * C
    slots = line_ref.shape[0]
    s = lax.axis_index("span")
    c = lax.axis_index("chord")
    right, left = lax.rem(c + 1, n), lax.rem(c + n - 1, n)
    above, below = s > 0, s < N - 1

    loads = [
        pltpu.make_async_copy(src, dst, load_sems.at[k])
        for k, (src, dst) in enumerate(
            (
                (right_hbm, right_ref),
                (scale_hbm, scale_ref),
                (extra_hbm, extra_ref),
                (line_hbm, line_ref),
                (partner_hbm, partner_ref),
            )
        )
    ]
    for load in loads:
        load.start()

    barrier = pltpu.get_barrier_semaphore()
    for d in range(1, n):
        pl.semaphore_signal(barrier, inc=1, device_id=(s, lax.rem(c + d, n)), device_id_type=MESH)
    for d in range(1, N):
        pl.semaphore_signal(barrier, inc=1, device_id=(lax.rem(s + d, N), c), device_id_type=MESH)

    @pl.when(above)
    def _():
        for side in (left, right):
            pl.semaphore_signal(barrier, inc=1, device_id=(s - 1, side), device_id_type=MESH)

    @pl.when(below)
    def _():
        for side in (left, right):
            pl.semaphore_signal(barrier, inc=1, device_id=(s + 1, side), device_id_type=MESH)

    @pl.when(jnp.logical_not(above))
    def _():
        for t in range(2):
            rim[t, 0] = jnp.zeros(rim.shape[2:], F32)
            corner[t, 0] = jnp.zeros(corner.shape[2:], F32)

    @pl.when(jnp.logical_not(below))
    def _():
        for t in range(2):
            rim[t, 1] = jnp.zeros(rim.shape[2:], F32)
            corner[t, 1] = jnp.zeros(corner.shape[2:], F32)

    offset = iota((L, L), 0) - iota((L, L), 1)
    band = jnp.concatenate([taps_at(offset, mass_taps), taps_at(offset, bend_taps)], axis=1)
    k_at, c_at = iota((2 * TILE, L), 0), iota((2 * TILE, L), 1)
    from_left = jnp.logical_and(k_at >= REACH, k_at < 2 * REACH)
    from_right = jnp.logical_and(k_at >= TILE, k_at < TILE + REACH)
    place = jnp.where(k_at < TILE, k_at - 2 * REACH, L + k_at - TILE)
    reach = jnp.where(jnp.logical_or(from_left, from_right), place - c_at, 2 * L)
    side_band = jnp.concatenate([taps_at(reach, mass_taps), taps_at(reach, bend_taps)], axis=1)
    h_at, hc_at = iota((TILE, L), 0), iota((TILE, L), 1)
    halo_line = jnp.where(h_at < REACH, h_at, L - 2 * REACH + h_at)
    halo_pick = jnp.where(
        jnp.logical_and(h_at < 2 * REACH, halo_line == hc_at), F32(1.0), F32(0.0)
    )

    for load in loads:
        load.wait()

    q_at, qc_at = iota((slots, L), 0), iota((slots, L), 1)
    j_at, jc_at = iota((n * slots, L), 0), iota((n * slots, L), 1)
    pick = jnp.zeros((slots, L), F32)
    spread = jnp.zeros((n * slots, L), F32)
    for q in range(slots):
        line, mate = line_ref[q], partner_ref[q]
        pick = jnp.where(jnp.logical_and(q_at == q, qc_at == line), F32(1.0), pick)
        owner = lax.div(mate, jnp.int32(slots))
        away = c - owner
        away = jnp.where(away < 0, away + n, away)
        at = away * slots + (mate - owner * slots)
        spread = jnp.where(jnp.logical_and(j_at == at, jc_at == line), F32(-penalty_weight), spread)
    on_line = jnp.sum(pick, axis=0, keepdims=True)

    scale = scale_ref[...][:, None, :]
    diag = (extra_ref[...] + F32(penalty_weight) * on_line)[:, None, :]

    basis[0] = jnp.swapaxes(right_ref[...], 0, 1)

    def remote(src, dst, sems, at, to):
        return pltpu.make_async_remote_copy(
            src_ref=src,
            dst_ref=dst,
            send_sem=sems.at[(0,) + at],
            recv_sem=sems.at[(1,) + at],
            device_id=to,
            device_id_type=MESH,
        )

    def flat(t):
        return basis[t].reshape(RC, L)

    def wide(t):
        return jnp.concatenate([basis[t, r] for r in range(R)], axis=1)

    def copies(t):
        down = [remote(weighted.at[t, pl.ds(R - REACH, REACH)], rim.at[t, 0], rim_sems, (t, 0), (s + 1, c))]
        up = [remote(weighted.at[t, pl.ds(0, REACH)], rim.at[t, 1], rim_sems, (t, 1), (s - 1, c))]
        last, first = pl.ds(RC - LANES, LANES), pl.ds(0, LANES)
        for k, to in enumerate((right, left)):
            spot = pl.ds(k * TILE, TILE)
            down.append(
                remote(halo_out.at[t, :, last], corner.at[t, 0, spot], corner_sems, (t, 0, k), (s + 1, to))
            )
            up.append(
                remote(halo_out.at[t, :, first], corner.at[t, 1, spot], corner_sems, (t, 1, k), (s - 1, to))
            )
        around = []
        for k, to in enumerate((right, left)):
            spot = pl.ds(k * TILE, TILE)
            around.append(remote(halo_out.at[t], halo.at[t, spot], halo_sems, (t, k), (s, to)))
        for d in range(1, n):
            around.append(
                remote(
                    iface.at[t, pl.ds(0, slots)],
                    iface.at[t, pl.ds(d * slots, slots)],
                    iface_sems,
                    (t, d),
                    (s, lax.rem(c + d, n)),
                )
            )
        return down, up, around

    def prepare(t):
        w = scale * basis[t]
        weighted[t] = w
        halo_out[t] = dot(halo_pick, w.reshape(RC, L), 1, 1)
        iface[t, 0:slots] = dot(pick, flat(t), 1, 1)

    def send(t):
        down, up, around = copies(t)

        @pl.when(below)
        def _():
            for copy in down:
                copy.start()

        @pl.when(above)
        def _():
            for copy in up:
                copy.start()

        for copy in around:
            copy.start()

    def inner(t):
        both = dot(weighted[t].reshape(RC, L), band, 1, 0)
        ext_m[REACH : REACH + R] = both[:, :L].reshape(R, C, L)
        ext_b[REACH : REACH + R] = both[:, L:].reshape(R, C, L)

    def receive(t):
        down, up, around = copies(t)

        @pl.when(above)
        def _():
            for copy in down:
                copy.wait_recv()

        @pl.when(below)
        def _():
            for copy in up:
                copy.wait_recv()

        for copy in around:
            copy.wait_recv()

    def sent(t):
        down, up, around = copies(t)

        @pl.when(below)
        def _():
            for copy in down:
                copy.wait_send()

        @pl.when(above)
        def _():
            for copy in up:
                copy.wait_send()

        for copy in around:
            copy.wait_send()

    def outer(t):
        edge = REACH * C
        ends = dot(rim[t].reshape(2 * edge, L), band, 1, 0)
        top = ends[:edge] + dot(corner[t, 0], side_band, 0, 0)[LANES - edge :]
        low = ends[edge:] + dot(corner[t, 1], side_band, 0, 0)[:edge]
        mid = dot(halo[t], side_band, 0, 0)
        ext_m[0:REACH] = top[:, :L].reshape(REACH, C, L)
        ext_b[0:REACH] = top[:, L:].reshape(REACH, C, L)
        ext_m[REACH + R :] = low[:, :L].reshape(REACH, C, L)
        ext_b[REACH + R :] = low[:, L:].reshape(REACH, C, L)
        ext_m[REACH : REACH + R] += mid[:, :L].reshape(R, C, L)
        ext_b[REACH : REACH + R] += mid[:, L:].reshape(R, C, L)
        y = span_sum(ext_m, bend_taps, R) + span_sum(ext_b, mass_taps, R)
        coupled = dot(iface[t], spread, 0, 0).reshape(R, C, L)
        basis[t + 1] = scale * y + diag * basis[t] + coupled

    def group_copies(buf, sems, which, count, to):
        return [remote(buf.at[0], buf.at[d], sems, (which, d), to(d)) for d in range(1, count)]

    def along_chord(d):
        return (s, lax.rem(c + d, n))

    def along_span(d):
        return (lax.rem(s + d, N), c)

    def total(buf, count):
        out = buf[0]
        for d in range(1, count):
            out = out + buf[d]
        return out

    def pad(x):
        return jnp.concatenate([x, jnp.zeros((x.shape[0], LANES - x.shape[1]), F32)], axis=1)

    ec = group_copies(early_c, chord_sems, 0, n, along_chord)
    es = group_copies(early_s, span_sems, 0, N, along_span)
    lc = group_copies(late_c, chord_sems, 1, n, along_chord)
    ls = group_copies(late_s, span_sems, 1, N, along_span)

    prepare(0)
    greeted = (n - 1) + (N - 1) + 2 * (above.astype(jnp.int32) + below.astype(jnp.int32))
    pl.semaphore_wait(barrier, greeted)
    send(0)
    inner(0)
    receive(0)
    outer(0)
    prepare(1)
    send(1)

    v0, v1 = wide(0), wide(1)
    first = exact_dot(v0, jnp.concatenate([v1, v0], axis=0), 1, 1)
    g11 = exact_dot(v1, v1, 1, 1)
    early_c[0] = pad(jnp.concatenate([first[:, :C], g11, first[:, C:]], axis=1))
    for copy in ec:
        copy.start()
    inner(1)
    for copy in ec:
        copy.wait_recv()
    early_s[0] = total(early_c, n)
    for copy in es:
        copy.start()
    receive(1)
    outer(1)
    late_c[0] = pad(exact_dot(wide(1), jnp.concatenate([wide(0), wide(2)], axis=0), 1, 1))
    for copy in lc:
        copy.start()
    for copy in es:
        copy.wait_recv()
    table = total(early_s, N)
    g01, g11 = table[:, :C], table[:, C : 2 * C]
    table = eliminate(table, 0, C)
    folded = exact_dot(g11, table, 1, 0)
    slope = table[:, C : 2 * C]
    step = table[:, 2 * C : 3 * C]
    lead = pad(jnp.concatenate([jnp.zeros((C, 2 * C), F32), g01], axis=1))
    rest = lead - folded
    for copy in lc:
        copy.wait_recv()
    late_s[0] = total(late_c, n)
    for copy in ls:
        copy.start()
    for copy in ls:
        copy.wait_recv()
    table = eliminate(rest + total(late_s, N), C, C)
    y1 = table[:, 2 * C : 3 * C]
    y0 = step - exact_dot(slope, y1, 1, 0)
    mix = jnp.concatenate([y0, y1], axis=0)

    v0, v1, v2 = wide(0), wide(1), wide(2)
    found = dot(mix, jnp.concatenate([v0, v1], axis=0), 0, 0)
    left_over = v0 - dot(mix, jnp.concatenate([v1, v2], axis=0), 0, 0)

    def narrow(x):
        rows = jnp.stack([x[:, r * L : (r + 1) * L] for r in range(R)], axis=0)
        return jnp.swapaxes(rows, 0, 1)

    solution_ref[...] = narrow(found)
    residual_ref[...] = narrow(left_over)
    sent(0)
    sent(1)
    for copy in ec + es + lc + ls:
        copy.wait_send()


def body(n, N, right_side, stiff_scale, extra_diag, iface_line, partner):
    C, R, L = right_side.shape
    slots = iface_line.shape[0]
    vmem = pl.BlockSpec(memory_space=pltpu.VMEM)
    hbm = pl.BlockSpec(memory_space=pltpu.HBM)
    dma = pltpu.SemaphoreType.DMA
    field = jax.ShapeDtypeStruct((C, R, L), F32)
    return pl.pallas_call(
        functools.partial(kernel, n, N),
        out_shape=(field, field),
        in_specs=[hbm] * 5,
        out_specs=(vmem, vmem),
        scratch_shapes=[
            pltpu.VMEM((C, R, L), F32),
            pltpu.VMEM((R, L), F32),
            pltpu.VMEM((R, L), F32),
            pltpu.SMEM((slots,), jnp.int32),
            pltpu.SMEM((slots,), jnp.int32),
            pltpu.VMEM((3, R, C, L), F32),
            pltpu.VMEM((2, R, C, L), F32),
            pltpu.VMEM((2, TILE, R * C), F32),
            pltpu.VMEM((2, 2 * TILE, R * C), F32),
            pltpu.VMEM((2, n * slots, R * C), F32),
            pltpu.VMEM((2, 2, REACH, C, L), F32),
            pltpu.VMEM((2, 2, 2 * TILE, LANES), F32),
            pltpu.VMEM((R + 2 * REACH, C, L), F32),
            pltpu.VMEM((R + 2 * REACH, C, L), F32),
            pltpu.VMEM((n, C, LANES), F32),
            pltpu.VMEM((N, C, LANES), F32),
            pltpu.VMEM((n, C, LANES), F32),
            pltpu.VMEM((N, C, LANES), F32),
            dma((2, 2, 2)),
            dma((2, 2, 2)),
            dma((2, 2, 2, 2)),
            dma((2, 2, n)),
            dma((2, 2, n)),
            dma((2, 2, N)),
            dma((5,)),
        ],
        compiler_params=pltpu.CompilerParams(
            collective_id=0, has_side_effects=True, vmem_limit_bytes=64 * 1024 * 1024
        ),
        name="shell_cg",
    )(right_side, stiff_scale, extra_diag, iface_line, partner)


def solution(mesh):
    sizes = dict(mesh.shape)
    return jax.shard_map(
        functools.partial(body, sizes["chord"], sizes["span"]),
        mesh=mesh,
        in_specs=(
            P(None, "span", "chord"),
            P("span", "chord"),
            P("span", "chord"),
            P("chord"),
            P("chord"),
        ),
        out_specs=(P(None, "span", "chord"), P(None, "span", "chord")),
        check_vma=False,
    )
```

profile of v0, /device:TPU:0, one launch (start us, length us, event | category | flops | bytes accessed | tf_op | source)
XLA Modules:
  0.0 29.3 jit_solution(691548474305488276)
XLA Ops:
  0.6 26.2 %shell_cg.1 = (f32[16,32,128]{2,1,0:T(8,128)}, f32[16,32,128]{2,1,0:T(8,128)}) custom-call(f32[16,32,128]{2,1,0:T(8,128)} %right_hbm.1, f32[32,128]{1,0:T(8,128)} %scale_hbm.1, f32[32,128]{1,0:T(8,128)} %extra_hbm.1, s32[8]{0:T(128)} %line_hbm.1, s32[8]{0:T(128)} %partner_hbm.1), custom_call_target="tpu_custom_call" | custom-call | tf_op jit(solution)/shard_map/shell_cg/pallas_call | solution.py:418
  26.8 0.0 copy-start
  26.9 1.7 %copy.9 = f32[16,32,128]{2,1,0:T(8,128)} copy(f32[16,32,128]{2,1,0:T(8,128)} %get-tuple-element.4) | data formatting | bytes 524288
  28.6 0.0 copy-done
  28.6 0.7 %copy.10 = f32[16,32,128]{2,1,0:T(8,128)} copy(f32[16,32,128]{2,1,0:T(8,128)S(1)} %copy-done) | data formatting | bytes 524288
Async XLA Ops:
  26.8 1.7 %copy-start = (f32[16,32,128]{2,1,0:T(8,128)S(1)}, f32[16,32,128]{2,1,0:T(8,128)}, u32[]{:S(2)}) copy-start(f32[16,32,128]{2,1,0:T(8,128)} %get-tuple-element.5) | copy-start | bytes 786436
where the time goes:
time: 29.4 us; the launch traced here: 29.3 us
  Pallas kernels  26.2 us (89%)
  local copies, waits for them, and re-layouts  2.42 us (8%)
  between operations  0.65 us (2%)
    pallas_call x1, Pallas kernels, body(): pl.pallas_call(functools.partial(kernel, n, N), out_shape=(field, field),...  26.2 us
    unnamed x4, local copies, waits for them, and re-layouts  2.42 us

commit v1 on v0

--- a/solution.py
+++ b/solution.py
@@ -7,16 +7,11 @@
 from jax.experimental.pallas import tpu as pltpu
 from jax.sharding import PartitionSpec as P
 
-mass_taps = (
-    1.0 / 5040.0,
-    120.0 / 5040.0,
-    1191.0 / 5040.0,
-    2416.0 / 5040.0,
-    1191.0 / 5040.0,
-    120.0 / 5040.0,
-    1.0 / 5040.0,
-)
-bend_taps = (1.0 / 6.0, 0.0, -1.5, 8.0 / 3.0, -1.5, 0.0, 1.0 / 6.0)
+mass_taps = (1.0, 120.0, 1191.0, 2416.0, 1191.0, 120.0, 1.0)
+mass_high = (1.0, 120.0, 1192.0, 2416.0, 1192.0, 120.0, 1.0)
+mass_low = (0.0, 0.0, -1.0, 0.0, -1.0, 0.0, 0.0)
+bend_taps = (1.0, 0.0, -9.0, 16.0, -9.0, 0.0, 1.0)
+tap_unit = 1.0 / (5040.0 * 6.0)
 penalty_weight = 4.0
 REACH = 3
 LANES = 128
@@ -33,6 +28,18 @@
         precision=precision,
         preferred_element_type=F32,
     )
+
+
+def product(a, b, a_dim, b_dim):
+    return lax.dot_general(a, b, (((a_dim,), (b_dim,)), ((), ())), preferred_element_type=F32)
+
+
+def split(x):
+    high = x.astype(jnp.bfloat16)
+    rest = x - high.astype(F32)
+    mid = rest.astype(jnp.bfloat16)
+    low = (rest - mid.astype(F32)).astype(jnp.bfloat16)
+    return high, mid, low
 
 
 exact_dot = functools.partial(dot, precision=lax.Precision.HIGHEST)
@@ -95,6 +102,8 @@
     partner_ref,
     basis,
     weighted,
+    terms,
+    w_terms,
     halo_out,
     halo,
     iface,
@@ -166,14 +175,21 @@
             corner[t, 1] = jnp.zeros(corner.shape[2:], F32)
 
     offset = iota((L, L), 0) - iota((L, L), 1)
-    band = jnp.concatenate([taps_at(offset, mass_taps), taps_at(offset, bend_taps)], axis=1)
+
+    def bands(at):
+        bend = taps_at(at, bend_taps)
+        high = jnp.concatenate([taps_at(at, mass_high), bend], axis=1)
+        low = jnp.concatenate([taps_at(at, mass_low), jnp.zeros_like(bend)], axis=1)
+        return jnp.concatenate([high, high, high, low], axis=0).astype(jnp.bfloat16)
+
+    band = bands(offset)
     k_at, c_at = iota((2 * TILE, L), 0), iota((2 * TILE, L), 1)
     from_left = jnp.logical_and(k_at >= REACH, k_at < 2 * REACH)
     from_right = jnp.logical_and(k_at >= TILE, k_at < TILE + REACH)
     place = jnp.where(k_at < TILE, k_at - 2 * REACH, L + k_at - TILE)
     reach = jnp.where(jnp.logical_or(from_left, from_right), place - c_at, 2 * L)
-    side_band = jnp.concatenate([taps_at(reach, mass_taps), taps_at(reach, bend_taps)], axis=1)
-    h_at, hc_at = iota((TILE, L), 0), iota((TILE, L), 1)
+    side_band = bands(reach)
+    h_at, hc_at = iota((2 * TILE, L), 0), iota((2 * TILE, L), 1)
     halo_line = jnp.where(h_at < REACH, h_at, L - 2 * REACH + h_at)
     halo_pick = jnp.where(
         jnp.logical_and(h_at < 2 * REACH, halo_line == hc_at), F32(1.0), F32(0.0)
@@ -182,9 +198,11 @@
     for load in loads:
         load.wait()
 
-    q_at, qc_at = iota((slots, L), 0), iota((slots, L), 1)
+    halo_pick = jnp.concatenate([halo_pick] * 3, axis=1).astype(jnp.bfloat16)
+
+    q_at, qc_at = iota((2 * TILE, L), 0), iota((2 * TILE, L), 1)
     j_at, jc_at = iota((n * slots, L), 0), iota((n * slots, L), 1)
-    pick = jnp.zeros((slots, L), F32)
+    pick = jnp.zeros((2 * TILE, L), F32)
     spread = jnp.zeros((n * slots, L), F32)
     for q in range(slots):
         line, mate = line_ref[q], partner_ref[q]
@@ -195,11 +213,11 @@
         at = away * slots + (mate - owner * slots)
         spread = jnp.where(jnp.logical_and(j_at == at, jc_at == line), F32(-penalty_weight), spread)
     on_line = jnp.sum(pick, axis=0, keepdims=True)
+    pick = jnp.concatenate([pick] * 3, axis=1).astype(jnp.bfloat16)
+    spread = jnp.concatenate([spread] * 3, axis=0).astype(jnp.bfloat16)
 
     scale = scale_ref[...][:, None, :]
     diag = (extra_ref[...] + F32(penalty_weight) * on_line)[:, None, :]
-
-    basis[0] = jnp.swapaxes(right_ref[...], 0, 1)
 
     def remote(src, dst, sems, at, to):
         return pltpu.make_async_remote_copy(
@@ -211,11 +229,17 @@
             device_id_type=MESH,
         )
 
-    def flat(t):
-        return basis[t].reshape(RC, L)
-
-    def wide(t):
-        return jnp.concatenate([basis[t, r] for r in range(R)], axis=1)
+    def keep(t, field):
+        basis[t] = field
+        for k, term in enumerate(split(field)):
+            terms[t, :, k * C : (k + 1) * C] = term
+
+    def wide(t, count=3):
+        return jnp.concatenate([terms[t, r, 0 : count * C] for r in range(R)], axis=1)
+
+    def stacked(x, axis):
+        high, mid, low = split(x)
+        return jnp.concatenate([high, mid, low, high], axis=axis)
 
     def copies(t):
         down = [remote(weighted.at[t, pl.ds(R - REACH, REACH)], rim.at[t, 0], rim_sems, (t, 0), (s + 1, c))]
@@ -248,8 +272,12 @@
     def prepare(t):
         w = scale * basis[t]
         weighted[t] = w
-        halo_out[t] = dot(halo_pick, w.reshape(RC, L), 1, 1)
-        iface[t, 0:slots] = dot(pick, flat(t), 1, 1)
+        w_terms[...] = stacked(w.reshape(RC, L), 1)
+        halo_out[t] = product(halo_pick, w_terms[:, 0 : 3 * L], 1, 1)[:TILE]
+        v = jnp.concatenate(
+            [terms[t, :, k * C : (k + 1) * C].reshape(RC, L) for k in range(3)], axis=1
+        )
+        iface[t, 0:slots] = product(pick, v, 1, 1)[:slots]
 
     def send(t):
         down, up, around = copies(t)
@@ -267,8 +295,8 @@
         for copy in around:
             copy.start()
 
-    def inner(t):
-        both = dot(weighted[t].reshape(RC, L), band, 1, 0)
+    def inner():
+        both = product(w_terms[...], band, 1, 0)
         ext_m[REACH : REACH + R] = both[:, :L].reshape(R, C, L)
         ext_b[REACH : REACH + R] = both[:, L:].reshape(R, C, L)
 
@@ -306,10 +334,10 @@
 
     def outer(t):
         edge = REACH * C
-        ends = dot(rim[t].reshape(2 * edge, L), band, 1, 0)
-        top = ends[:edge] + dot(corner[t, 0], side_band, 0, 0)[LANES - edge :]
-        low = ends[edge:] + dot(corner[t, 1], side_band, 0, 0)[:edge]
-        mid = dot(halo[t], side_band, 0, 0)
+        ends = product(stacked(rim[t].reshape(2 * edge, L), 1), band, 1, 0)
+        top = ends[:edge] + product(stacked(corner[t, 0], 0), side_band, 0, 0)[LANES - edge :]
+        low = ends[edge:] + product(stacked(corner[t, 1], 0), side_band, 0, 0)[:edge]
+        mid = product(stacked(halo[t], 0), side_band, 0, 0)
         ext_m[0:REACH] = top[:, :L].reshape(REACH, C, L)
         ext_b[0:REACH] = top[:, L:].reshape(REACH, C, L)
         ext_m[REACH + R :] = low[:, :L].reshape(REACH, C, L)
@@ -317,8 +345,9 @@
         ext_m[REACH : REACH + R] += mid[:, :L].reshape(R, C, L)
         ext_b[REACH : REACH + R] += mid[:, L:].reshape(R, C, L)
         y = span_sum(ext_m, bend_taps, R) + span_sum(ext_b, mass_taps, R)
-        coupled = dot(iface[t], spread, 0, 0).reshape(R, C, L)
-        basis[t + 1] = scale * y + diag * basis[t] + coupled
+        lines = jnp.concatenate(split(iface[t]), axis=0)
+        coupled = product(lines, spread, 0, 0).reshape(R, C, L)
+        keep(t + 1, (scale * F32(tap_unit)) * y + diag * basis[t] + coupled)
 
     def group_copies(buf, sems, which, count, to):
         return [remote(buf.at[0], buf.at[d], sems, (which, d), to(d)) for d in range(1, count)]
@@ -343,23 +372,30 @@
     lc = group_copies(late_c, chord_sems, 1, n, along_chord)
     ls = group_copies(late_s, span_sems, 1, N, along_span)
 
+    def gram(table, i, j):
+        block = table[3 * C * i : 3 * C * (i + 1), 3 * C * j : 3 * C * (j + 1)]
+        rows = block[:C] + block[C : 2 * C] + block[2 * C :]
+        return rows[:, :C] + rows[:, C : 2 * C] + rows[:, 2 * C :]
+
+    keep(0, jnp.swapaxes(right_ref[...], 0, 1))
     prepare(0)
     greeted = (n - 1) + (N - 1) + 2 * (above.astype(jnp.int32) + below.astype(jnp.int32))
     pl.semaphore_wait(barrier, greeted)
     send(0)
-    inner(0)
+    inner()
     receive(0)
     outer(0)
     prepare(1)
     send(1)
 
-    v0, v1 = wide(0), wide(1)
-    first = exact_dot(v0, jnp.concatenate([v1, v0], axis=0), 1, 1)
-    g11 = exact_dot(v1, v1, 1, 1)
-    early_c[0] = pad(jnp.concatenate([first[:, :C], g11, first[:, C:]], axis=1))
+    pair = jnp.concatenate([wide(0), wide(1)], axis=0)
+    early = product(pair, pair, 1, 1)
+    early_c[0] = pad(
+        jnp.concatenate([gram(early, 0, 1), gram(early, 1, 1), gram(early, 0, 0)], axis=1)
+    )
     for copy in ec:
         copy.start()
-    inner(1)
+    inner()
     for copy in ec:
         copy.wait_recv()
     early_s[0] = total(early_c, n)
@@ -367,7 +403,8 @@
         copy.start()
     receive(1)
     outer(1)
-    late_c[0] = pad(exact_dot(wide(1), jnp.concatenate([wide(0), wide(2)], axis=0), 1, 1))
+    late = gram(product(wide(1), wide(2), 1, 1), 0, 0)
+    late_c[0] = pad(jnp.concatenate([jnp.zeros((C, C), F32), late], axis=1))
     for copy in lc:
         copy.start()
     for copy in es:
@@ -390,11 +427,18 @@
     table = eliminate(rest + total(late_s, N), C, C)
     y1 = table[:, 2 * C : 3 * C]
     y0 = step - exact_dot(slope, y1, 1, 0)
-    mix = jnp.concatenate([y0, y1], axis=0)
-
-    v0, v1, v2 = wide(0), wide(1), wide(2)
-    found = dot(mix, jnp.concatenate([v0, v1], axis=0), 0, 0)
-    left_over = v0 - dot(mix, jnp.concatenate([v1, v2], axis=0), 0, 0)
+    (a0, b0, c0), (a1, b1, c1) = split(y0), split(y1)
+    mix = jnp.concatenate([a0, a0, a0, a1, a1, a1, b0, b0, b1, b1, c0, c1], axis=0)
+
+    def mixed(i, j):
+        field = jnp.concatenate(
+            [wide(i), wide(j), wide(i, 2), wide(j, 2), wide(i, 1), wide(j, 1)], axis=0
+        )
+        return product(mix, field, 0, 0)
+
+    found = mixed(0, 1)
+    start = jnp.concatenate([basis[0, r] for r in range(R)], axis=1)
+    left_over = start - mixed(1, 2)
 
     def narrow(x):
         rows = jnp.stack([x[:, r * L : (r + 1) * L] for r in range(R)], axis=0)
@@ -428,6 +472,8 @@
             pltpu.SMEM((slots,), jnp.int32),
             pltpu.VMEM((3, R, C, L), F32),
             pltpu.VMEM((2, R, C, L), F32),
+            pltpu.VMEM((3, R, 3 * C, L), jnp.bfloat16),
+            pltpu.VMEM((R * C, 4 * L), jnp.bfloat16),
             pltpu.VMEM((2, TILE, R * C), F32),
             pltpu.VMEM((2, 2 * TILE, R * C), F32),
             pltpu.VMEM((2, n * slots, R * C), F32),
@@ -448,7 +494,7 @@
             dma((5,)),
         ],
         compiler_params=pltpu.CompilerParams(
-            collective_id=0, has_side_effects=True, vmem_limit_bytes=64 * 1024 * 1024
+            collective_id=0, has_side_effects=True, vmem_limit_bytes=64 * 1024 * 1024 - 2 * 4 * C * R * L
         ),
         name="shell_cg",
     )(right_side, stiff_scale, extra_diag, iface_line, partner)

time: 29.4 us -> 28.3 us (0.963)
  Pallas kernels: 26.2 us -> 25.1 us
    pallas_call x1, Pallas kernels: 26.2 us -> 25.1 us  [body(): pl.pallas_call(functools.partial(kernel, n, N), out_shape=(field, field),...]
where the time goes in v1:
time: 28.3 us; the launch traced here: 28.2 us
  Pallas kernels  25.1 us (89%)
  local copies, waits for them, and re-layouts  2.42 us (9%)
  between operations  0.65 us (2%)
    pallas_call x1, Pallas kernels, body(): pl.pallas_call(functools.partial(kernel, n, N), out_shape=(field, field),...  25.1 us
    unnamed x4, local copies, waits for them, and re-layouts  2.42 us

profile of v1, /device:TPU:0, one launch (start us, length us, event | category | flops | bytes accessed | tf_op | source)
XLA Modules:
  0.0 28.2 jit_solution(11546047957966984439)
XLA Ops:
  0.6 25.1 %shell_cg.1 = (f32[16,32,128]{2,1,0:T(8,128)}, f32[16,32,128]{2,1,0:T(8,128)}) custom-call(f32[16,32,128]{2,1,0:T(8,128)} %right_hbm.1, f32[32,128]{1,0:T(8,128)} %scale_hbm.1, f32[32,128]{1,0:T(8,128)} %extra_hbm.1, s32[8]{0:T(128)} %line_hbm.1, s32[8]{0:T(128)} %partner_hbm.1), custom_call_target="tpu_custom_call" | custom-call | tf_op jit(solution)/shard_map/shell_cg/pallas_call | solution.py:462
  25.7 0.0 copy-start
  25.7 1.7 %copy.9 = f32[16,32,128]{2,1,0:T(8,128)} copy(f32[16,32,128]{2,1,0:T(8,128)} %get-tuple-element.4) | data formatting | bytes 524288
  27.5 0.0 copy-done
  27.5 0.7 %copy.10 = f32[16,32,128]{2,1,0:T(8,128)} copy(f32[16,32,128]{2,1,0:T(8,128)S(1)} %copy-done) | data formatting | bytes 524288
Async XLA Ops:
  25.7 1.7 %copy-start = (f32[16,32,128]{2,1,0:T(8,128)S(1)}, f32[16,32,128]{2,1,0:T(8,128)}, u32[]{:S(2)}) copy-start(f32[16,32,128]{2,1,0:T(8,128)} %get-tuple-element.5) | copy-start | bytes 786436

commit v2 on v1

--- a/solution.py
+++ b/solution.py
@@ -378,31 +378,41 @@
         return rows[:, :C] + rows[:, C : 2 * C] + rows[:, 2 * C :]
 
     keep(0, jnp.swapaxes(right_ref[...], 0, 1))
-    prepare(0)
     greeted = (n - 1) + (N - 1) + 2 * (above.astype(jnp.int32) + below.astype(jnp.int32))
-    pl.semaphore_wait(barrier, greeted)
-    send(0)
-    inner()
-    receive(0)
-    outer(0)
-    prepare(1)
-    send(1)
-
-    pair = jnp.concatenate([wide(0), wide(1)], axis=0)
-    early = product(pair, pair, 1, 1)
-    early_c[0] = pad(
-        jnp.concatenate([gram(early, 0, 1), gram(early, 1, 1), gram(early, 0, 0)], axis=1)
-    )
-    for copy in ec:
-        copy.start()
-    inner()
-    for copy in ec:
-        copy.wait_recv()
-    early_s[0] = total(early_c, n)
-    for copy in es:
-        copy.start()
-    receive(1)
-    outer(1)
+
+    @pl.loop(0, 2)
+    def _(t):
+        prepare(t)
+
+        @pl.when(t == 0)
+        def _():
+            pl.semaphore_wait(barrier, greeted)
+
+        send(t)
+
+        @pl.when(t == 1)
+        def _():
+            pair = jnp.concatenate([wide(0), wide(1)], axis=0)
+            early = product(pair, pair, 1, 1)
+            early_c[0] = pad(
+                jnp.concatenate([gram(early, 0, 1), gram(early, 1, 1), gram(early, 0, 0)], axis=1)
+            )
+            for copy in ec:
+                copy.start()
+
+        inner()
+
+        @pl.when(t == 1)
+        def _():
+            for copy in ec:
+                copy.wait_recv()
+            early_s[0] = total(early_c, n)
+            for copy in es:
+                copy.start()
+
+        receive(t)
+        outer(t)
+
     late = gram(product(wide(1), wide(2), 1, 1), 0, 0)
     late_c[0] = pad(jnp.concatenate([jnp.zeros((C, C), F32), late], axis=1))
     for copy in lc:
@@ -458,7 +468,7 @@
     vmem = pl.BlockSpec(memory_space=pltpu.VMEM)
     hbm = pl.BlockSpec(memory_space=pltpu.HBM)
     dma = pltpu.SemaphoreType.DMA
-    field = jax.ShapeDtypeStruct((C, R, L), F32)
+    field = pltpu.VMEM((C, R, L), F32)
     return pl.pallas_call(
         functools.partial(kernel, n, N),
         out_shape=(field, field),
@@ -494,7 +504,7 @@
             dma((5,)),
         ],
         compiler_params=pltpu.CompilerParams(
-            collective_id=0, has_side_effects=True, vmem_limit_bytes=64 * 1024 * 1024 - 2 * 4 * C * R * L
+            collective_id=0, has_side_effects=True, vmem_limit_bytes=60 * 1024 * 1024
         ),
         name="shell_cg",
     )(right_side, stiff_scale, extra_diag, iface_line, partner)

time: 28.3 us -> 26.4 us (0.933)
  local copies, waits for them, and re-layouts: 2.42 us -> 1.41 us
  Pallas kernels: 25.1 us -> 24.2 us
    unnamed x4 -> x2, local copies, waits for them, and re-layouts: 2.42 us -> 1.41 us
    pallas_call x1, Pallas kernels: 25.1 us -> 24.2 us  [body(): pl.pallas_call(functools.partial(kernel, n, N), out_shape=(field, field),...]
where the time goes in v2:
time: 26.4 us; the launch traced here: 26.3 us
  Pallas kernels  24.2 us (92%)
  local copies, waits for them, and re-layouts  1.41 us (5%)
  between operations  0.64 us (2%)
    pallas_call x1, Pallas kernels, body(): pl.pallas_call(functools.partial(kernel, n, N), out_shape=(field, field),...  24.2 us
    unnamed x2, local copies, waits for them, and re-layouts  1.41 us

profile of v2, /device:TPU:0, one launch (start us, length us, event | category | flops | bytes accessed | tf_op | source)
XLA Modules:
  0.0 26.3 jit_solution(18223724400305917797)
XLA Ops:
  0.6 24.2 %shell_cg.1 = (f32[16,32,128]{2,1,0:T(8,128)S(1)}, f32[16,32,128]{2,1,0:T(8,128)S(1)}) custom-call(f32[16,32,128]{2,1,0:T(8,128)} %right_hbm.1, f32[32,128]{1,0:T(8,128)} %scale_hbm.1, f32[32,128]{1,0:T(8,128)} %extra_hbm.1, s32[8]{0:T(128)} %line_hbm.1, s32[8]{0:T(128)} %partner_hbm.1), custom_call_target="tpu_custom_call" | custom-call | tf_op jit(solution)/shard_map/shell_cg/pallas_call | solution.py:472
  24.9 0.7 %copy.9 = f32[16,32,128]{2,1,0:T(8,128)} copy(f32[16,32,128]{2,1,0:T(8,128)S(1)} %get-tuple-element.2) | data formatting | bytes 524288
  25.6 0.7 %copy.10 = f32[16,32,128]{2,1,0:T(8,128)} copy(f32[16,32,128]{2,1,0:T(8,128)S(1)} %get-tuple-element.3) | data formatting | bytes 524288

commit v3 on v2

--- a/solution.py
+++ b/solution.py
@@ -257,8 +257,9 @@
         for k, to in enumerate((right, left)):
             spot = pl.ds(k * TILE, TILE)
             around.append(remote(halo_out.at[t], halo.at[t, spot], halo_sems, (t, k), (s, to)))
+        lines = []
         for d in range(1, n):
-            around.append(
+            lines.append(
                 remote(
                     iface.at[t, pl.ds(0, slots)],
                     iface.at[t, pl.ds(d * slots, slots)],
@@ -267,20 +268,22 @@
                     (s, lax.rem(c + d, n)),
                 )
             )
-        return down, up, around
+        return down, up, around, lines
 
     def prepare(t):
         w = scale * basis[t]
         weighted[t] = w
         w_terms[...] = stacked(w.reshape(RC, L), 1)
         halo_out[t] = product(halo_pick, w_terms[:, 0 : 3 * L], 1, 1)[:TILE]
+
+    def prepare_lines(t):
         v = jnp.concatenate(
             [terms[t, :, k * C : (k + 1) * C].reshape(RC, L) for k in range(3)], axis=1
         )
         iface[t, 0:slots] = product(pick, v, 1, 1)[:slots]
 
     def send(t):
-        down, up, around = copies(t)
+        down, up, around, lines = copies(t)
 
         @pl.when(below)
         def _():
@@ -293,6 +296,9 @@
                 copy.start()
 
         for copy in around:
+            copy.start()
+        prepare_lines(t)
+        for copy in lines:
             copy.start()
 
     def inner():
@@ -300,8 +306,24 @@
         ext_m[REACH : REACH + R] = both[:, :L].reshape(R, C, L)
         ext_b[REACH : REACH + R] = both[:, L:].reshape(R, C, L)
 
-    def receive(t):
-        down, up, around = copies(t)
+    def sent(t):
+        down, up, around, lines = copies(t)
+
+        @pl.when(below)
+        def _():
+            for copy in down:
+                copy.wait_send()
+
+        @pl.when(above)
+        def _():
+            for copy in up:
+                copy.wait_send()
+
+        for copy in around + lines:
+            copy.wait_send()
+
+    def outer(t):
+        down, up, around, lines = copies(t)
 
         @pl.when(above)
         def _():
@@ -313,40 +335,24 @@
             for copy in up:
                 copy.wait_recv()
 
-        for copy in around:
-            copy.wait_recv()
-
-    def sent(t):
-        down, up, around = copies(t)
-
-        @pl.when(below)
-        def _():
-            for copy in down:
-                copy.wait_send()
-
-        @pl.when(above)
-        def _():
-            for copy in up:
-                copy.wait_send()
-
-        for copy in around:
-            copy.wait_send()
-
-    def outer(t):
         edge = REACH * C
         ends = product(stacked(rim[t].reshape(2 * edge, L), 1), band, 1, 0)
         top = ends[:edge] + product(stacked(corner[t, 0], 0), side_band, 0, 0)[LANES - edge :]
         low = ends[edge:] + product(stacked(corner[t, 1], 0), side_band, 0, 0)[:edge]
-        mid = product(stacked(halo[t], 0), side_band, 0, 0)
         ext_m[0:REACH] = top[:, :L].reshape(REACH, C, L)
         ext_b[0:REACH] = top[:, L:].reshape(REACH, C, L)
         ext_m[REACH + R :] = low[:, :L].reshape(REACH, C, L)
         ext_b[REACH + R :] = low[:, L:].reshape(REACH, C, L)
+        for copy in around:
+            copy.wait_recv()
+        mid = product(stacked(halo[t], 0), side_band, 0, 0)
         ext_m[REACH : REACH + R] += mid[:, :L].reshape(R, C, L)
         ext_b[REACH : REACH + R] += mid[:, L:].reshape(R, C, L)
         y = span_sum(ext_m, bend_taps, R) + span_sum(ext_b, mass_taps, R)
-        lines = jnp.concatenate(split(iface[t]), axis=0)
-        coupled = product(lines, spread, 0, 0).reshape(R, C, L)
+        for copy in lines:
+            copy.wait_recv()
+        every = jnp.concatenate(split(iface[t]), axis=0)
+        coupled = product(every, spread, 0, 0).reshape(R, C, L)
         keep(t + 1, (scale * F32(tap_unit)) * y + diag * basis[t] + coupled)
 
     def group_copies(buf, sems, which, count, to):
@@ -410,7 +416,6 @@
             for copy in es:
                 copy.start()
 
-        receive(t)
         outer(t)
 
     late = gram(product(wide(1), wide(2), 1, 1), 0, 0)
@@ -422,16 +427,16 @@
     table = total(early_s, N)
     g01, g11 = table[:, :C], table[:, C : 2 * C]
     table = eliminate(table, 0, C)
+    for copy in lc:
+        copy.wait_recv()
+    late_s[0] = total(late_c, n)
+    for copy in ls:
+        copy.start()
     folded = exact_dot(g11, table, 1, 0)
     slope = table[:, C : 2 * C]
     step = table[:, 2 * C : 3 * C]
     lead = pad(jnp.concatenate([jnp.zeros((C, 2 * C), F32), g01], axis=1))
     rest = lead - folded
-    for copy in lc:
-        copy.wait_recv()
-    late_s[0] = total(late_c, n)
-    for copy in ls:
-        copy.start()
     for copy in ls:
         copy.wait_recv()
     table = eliminate(rest + total(late_s, N), C, C)

time: 26.4 us -> 26.8 us (1.015)
  Pallas kernels: 24.2 us -> 24.6 us
    pallas_call x1, Pallas kernels: 24.2 us -> 24.6 us  [body(): pl.pallas_call(functools.partial(kernel, n, N), out_shape=(field, field),...]
where the time goes in v3:
time: 26.8 us; the launch traced here: 26.7 us
  Pallas kernels  24.6 us (92%)
  local copies, waits for them, and re-layouts  1.41 us (5%)
  between operations  0.64 us (2%)
    pallas_call x1, Pallas kernels, body(): pl.pallas_call(functools.partial(kernel, n, N), out_shape=(field, field),...  24.6 us
    unnamed x2, local copies, waits for them, and re-layouts  1.41 us

profile of v3, /device:TPU:0, one launch (start us, length us, event | category | flops | bytes accessed | tf_op | source)
XLA Modules:
  0.0 26.7 jit_solution(8206254717979952461)
XLA Ops:
  0.6 24.6 %shell_cg.1 = (f32[16,32,128]{2,1,0:T(8,128)S(1)}, f32[16,32,128]{2,1,0:T(8,128)S(1)}) custom-call(f32[16,32,128]{2,1,0:T(8,128)} %right_hbm.1, f32[32,128]{1,0:T(8,128)} %scale_hbm.1, f32[32,128]{1,0:T(8,128)} %extra_hbm.1, s32[8]{0:T(128)} %line_hbm.1, s32[8]{0:T(128)} %partner_hbm.1), custom_call_target="tpu_custom_call" | custom-call | tf_op jit(solution)/shard_map/shell_cg/pallas_call | solution.py:477
  25.3 0.7 %copy.9 = f32[16,32,128]{2,1,0:T(8,128)} copy(f32[16,32,128]{2,1,0:T(8,128)S(1)} %get-tuple-element.2) | data formatting | bytes 524288
  26.0 0.7 %copy.10 = f32[16,32,128]{2,1,0:T(8,128)} copy(f32[16,32,128]{2,1,0:T(8,128)S(1)} %get-tuple-element.3) | data formatting | bytes 524288
